TPU v7x, 32 devices: a whole 2x2x4 slice. The times are simulated.
32 devices in a mesh: cd: 4 (over y, x), ab: 8 (over z, core).
Axes of the slice: x: 2, y: 2, z: 4, core: 2. Of those that a mesh axis runs over, the one named last changes fastest.
Arguments:
- amplitudes: float32 [2048, 16384], P('ab', 'cd'), may hold values from -6 to 6
- amp_tiles: int32 [16, 16], P('ab', 'cd'), may hold values 0 or 1
- integrals: float32 [16384, 16384], P('cd', 'ab'), may hold values from -0.046875 to 0.046875
- int_tiles: int32 [16, 16], P('cd', 'ab'), may hold values 0 or 1
- owner_tiles: int32 [16], replicated, may hold values from 0 to 15, each once
- other_terms: float32 [2048, 16384], P('cd', 'ab'), may hold values from -6 to 6
- denominators: float32 [2048, 16384], P('cd', 'ab'), may hold values from -4 to -0.5
Outputs:
- update: float32 [2048, 16384], P('cd', 'ab')
Inputs may be any that keep to these rules, and one draw needn't show every extreme that they name: owner_tiles is a permutation of the row tiles.
All inputs are finite; a program needn't handle non-finite values. No bound on the sum of `amp_tiles` or of `int_tiles` on one device may be relied on, other than what follows from the above.
Results may differ from a plain program's by a relative error of at most 0.00013.
Values sent between devices are 32-bit elements; how exact they have to be, the bound alone decides.
No kernel may reach another device: no remote copies, remote signals or barrier semaphores. Data moves between devices by JAX's collectives and lax.ppermute only.
A program may use at most 256 MiB of HBM per device.

v0:
```python
import functools

import jax
import jax.numpy as jnp
from jax import lax
from jax.experimental import pallas as pl
from jax.experimental.pallas import tpu as pltpu
from jax.sharding import PartitionSpec as P

TILE = 1024
TILE_ROWS = 128
CORES = 2
VMEM_BYTES = 58 * 1024 * 1024
COLUMNS = 256
ROUNDS = 4
FIRST, AWAY, STAY, WHOSE = 0, 2, 4, 6
CHAINS = 2
RANKS = (((0, 2), (1, 3)), ((0, 1), (2, 3)))


def spread_tiles(tile_flags, row_span, col_span):
    tile_rows, tile_cols = tile_flags.shape
    values = tile_flags.astype(jnp.float32)
    return jnp.broadcast_to(
        values[:, None, :, None], (tile_rows, row_span, tile_cols, col_span)
    ).reshape(tile_rows * row_span, tile_cols * col_span)


def plain(amplitudes, amp_tiles, integrals, int_tiles, owner_tiles, other_terms, denominators):
    masked_ints = integrals * spread_tiles(int_tiles, TILE, TILE)
    masked_amps = amplitudes * spread_tiles(amp_tiles, TILE_ROWS, TILE)
    tile_count = owner_tiles.shape[0]
    gathered = lax.all_gather(masked_amps, "ab", axis=0, tiled=True)
    partial_value = jnp.dot(
        gathered, masked_ints, precision=lax.Precision.HIGHEST, preferred_element_type=jnp.float32
    )
    col_width = partial_value.shape[1]
    partial_value = partial_value.reshape(tile_count, TILE_ROWS, col_width)[owner_tiles].reshape(
        tile_count * TILE_ROWS, col_width
    )
    owned = lax.psum_scatter(partial_value, "cd", scatter_dimension=0, tiled=True)
    return (owned + other_terms) / denominators


def plan_kernel(devices, half, owner_ref, here_ref, take_ref, source_ref, slot_ref, tile_ref, *scratch):
    inverse_ref, color_ref, pair_ref, device_ref, late_ref = scratch
    rank, spot = here_ref[0], here_ref[1]
    ranks = devices * 2 // ROUNDS
    for q in range(2 * devices):
        inverse_ref[owner_ref[q]] = q
        color_ref[q] = -1
    for d in range(devices):
        late_ref[d] = -1

    def walk(first, colors_ref, after):
        def step(state):
            at, _ = state
            colors_ref[at] = 0
            colors_ref[at ^ 1] = 1
            following = after(at ^ 1)
            return following, colors_ref[following]

        lax.while_loop(lambda state: state[1] < 0, step, (jnp.int32(first), colors_ref[first]))

    for t in range(0, 2 * devices, 2):
        walk(t, color_ref, lambda u: owner_ref[inverse_ref[u] ^ 1])
    for c in range(ranks):
        for p in range(2):
            q = ROUNDS * c + 2 * p
            second = color_ref[owner_ref[q]]
            source_ref[p * ranks + (c ^ rank)] = owner_ref[q + second] >> 1
            tile_ref[p * ranks + (c ^ rank)] = owner_ref[q + second]
            group = 2 * c + p
            device = owner_ref[q + 1 - second] >> 1
            device_ref[group] = device
            pair_ref[device] = group

            @pl.when(rank == c)
            def _():
                slot_ref[p] = 2 * p + second
                slot_ref[2 + p] = 2 * p + 1 - second

    for d in range(0, devices, 2):
        walk(d, late_ref, lambda u: device_ref[pair_ref[u] ^ 1])
    for c in range(ranks):
        swap = late_ref[device_ref[2 * c]]
        for p in range(2):
            r = 2 + (swap ^ p)
            device = device_ref[2 * c + p]
            source_ref[r * ranks + (c ^ rank)] = device >> 1
            tile_ref[r * ranks + (c ^ rank)] = 2 * device + 1 - color_ref[2 * device]

        @pl.when(jnp.logical_and(rank == c, swap != 0))
        def _():
            kept = slot_ref[2]
            slot_ref[2] = slot_ref[3]
            slot_ref[3] = kept

    early = color_ref[2 * spot]
    core = spot % CORES
    take_ref[FIRST] = early
    take_ref[FIRST + 1] = 0
    take_ref[AWAY] = 1 - early
    take_ref[AWAY + 1] = (1 - core) * half
    take_ref[STAY] = 1 - early
    take_ref[STAY + 1] = core * half
    take_ref[WHOSE] = late_ref[spot]


def plan(owner_tiles, here, devices, half):
    tiles = 2 * devices
    smem = pl.BlockSpec(memory_space=pltpu.SMEM)
    ints = jnp.int32
    return pl.pallas_call(
        functools.partial(plan_kernel, devices, half),
        out_shape=(
            jax.ShapeDtypeStruct((WHOSE + 1,), ints),
            jax.ShapeDtypeStruct((tiles,), ints),
            jax.ShapeDtypeStruct((ROUNDS,), ints),
            jax.ShapeDtypeStruct((tiles,), ints),
        ),
        in_specs=[smem, smem],
        out_specs=(smem, smem, smem, smem),
        scratch_shapes=[pltpu.SMEM((tiles,), ints)] * 2 + [pltpu.SMEM((devices,), ints)] * 3,
    )(owner_tiles, here)


def take_kernel(at, take_ref, flag_ref, amp_ref, out_ref):
    flag = flag_ref[take_ref[at], take_ref[at + 1] + pl.program_id(0)]
    out_ref[...] = amp_ref[...] * flag.astype(jnp.float32)


def take(at, tiles, where, amp_tiles, amplitudes):
    return pl.pallas_call(
        functools.partial(take_kernel, at),
        out_shape=jax.ShapeDtypeStruct((TILE_ROWS, tiles * TILE), jnp.float32),
        grid_spec=pltpu.PrefetchScalarGridSpec(
            num_scalar_prefetch=2,
            grid=(tiles,),
            in_specs=[
                pl.BlockSpec((TILE_ROWS, TILE), lambda j, where, flags: (where[at], where[at + 1] + j))
            ],
            out_specs=pl.BlockSpec((TILE_ROWS, TILE), lambda j, where, flags: (0, j)),
        ),
    )(where, amp_tiles, amplitudes)


def split_kernel(value_ref, halves_ref):
    value = value_ref[...]
    high = value.astype(jnp.bfloat16)
    halves_ref[:TILE, :] = high
    halves_ref[TILE:, :] = (value - high.astype(jnp.float32)).astype(jnp.bfloat16)


def split(integrals):
    depth, width = integrals.shape
    return pl.pallas_call(
        split_kernel,
        out_shape=jax.ShapeDtypeStruct((2 * depth, width), jnp.bfloat16),
        grid=(depth // TILE, width // TILE),
        in_specs=[pl.BlockSpec((TILE, TILE), lambda i, j: (i, j))],
        out_specs=pl.BlockSpec((2 * TILE, TILE), lambda i, j: (i, j)),
        compiler_params=pltpu.CompilerParams(vmem_limit_bytes=VMEM_BYTES),
        cost_estimate=pl.CostEstimate(flops=0, bytes_accessed=8 * depth * width, transcendentals=0),
    )(integrals)


def product_kernel(r, first, ranks, source_ref, tile_ref, row_flag_ref, flag_ref, amp_ref, halves_ref, *refs):
    out_refs, (tiles_ref, twice_ref, low_ref, total_ref, count_ref, row_ref, ready) = (
        refs[: 2 * CHAINS],
        refs[2 * CHAINS :],
    )
    width = halves_ref.shape[1]
    depth = low_ref.shape[1] // TILE
    step = pl.program_id(0)

    @pl.when(step == 0)
    def _():
        shards, _, wide = tiles_ref.shape[1:]
        copies = []
        for i in range(ranks):
            shard = pl.ds(source_ref[r * ranks + i] * shards, shards)
            copies.append(pltpu.make_async_copy(amp_ref.at[shard], tiles_ref.at[i], ready.at[i]))
            copies[i].start()
        for k in range(depth):
            count_ref[k] = 0
        for i in range(ranks):
            copies[i].wait()
            for shard in range(shards):
                for tile in range(wide // TILE):
                    k = shard * (wide // TILE) + tile

                    @pl.when(row_flag_ref[tile_ref[r * ranks + i], k] != 0)
                    def _():
                        count = count_ref[k]
                        row_ref[k * ranks + count] = i
                        count_ref[k] = count + 1
                        rows = pl.ds(pl.multiple_of(count * TILE_ROWS, TILE_ROWS), TILE_ROWS)
                        value = tiles_ref[i, shard, :, pl.ds(tile * TILE, TILE)]
                        high = value.astype(jnp.bfloat16)
                        twice_ref[rows, pl.ds(2 * k * TILE, TILE)] = high
                        twice_ref[rows, pl.ds((2 * k + 1) * TILE, TILE)] = high
                        low_ref[rows, pl.ds(k * TILE, TILE)] = (value - high.astype(jnp.float32)).astype(
                            jnp.bfloat16
                        )

    total_ref[...] = jnp.zeros_like(total_ref)

    @pl.loop(0, depth)
    def _(k):
        needed = flag_ref[k, (first + step) * width // TILE] != 0
        here = pl.ds(pl.multiple_of(k * TILE, TILE), TILE)
        top = pl.ds(pl.multiple_of(2 * k * TILE, TILE), TILE)
        deep = pl.ds(pl.multiple_of(2 * k * TILE, TILE), 2 * TILE)
        for count in range(1, ranks + 1):

            @pl.when(jnp.logical_and(needed, count_ref[k] == count))
            def _():
                rows = pl.ds(0, count * TILE_ROWS)
                part = jnp.dot(low_ref[rows, here], halves_ref[top, :], preferred_element_type=jnp.float32)
                part = part + jnp.dot(
                    twice_ref[rows, deep], halves_ref[deep, :], preferred_element_type=jnp.float32
                )
                for j in range(count):
                    at = pl.ds(pl.multiple_of(row_ref[k * ranks + j] * TILE_ROWS, TILE_ROWS), TILE_ROWS)
                    total_ref[at, :] += part[j * TILE_ROWS : (j + 1) * TILE_ROWS]

    share = width // CHAINS
    for chain, (kept, sent) in enumerate(RANKS):
        columns = pl.ds(chain * share, share)
        for ref, peers in ((out_refs[2 * chain], kept), (out_refs[2 * chain + 1], sent)):
            for i, peer in enumerate(peers):
                ref[i] = total_ref[pl.ds(peer * TILE_ROWS, TILE_ROWS), columns]


def product(r, first, steps, ranks, source, tile, row_flags, int_tiles, gathered, halves):
    depth, width = halves.shape[0] // 2, halves.shape[1]
    shards = depth // gathered.shape[2]
    rows = ranks * TILE_ROWS
    share = COLUMNS // CHAINS

    integral = pl.BlockSpec((2 * depth, COLUMNS), lambda i, *_: (0, first + i))
    return pl.pallas_call(
        functools.partial(product_kernel, r, first, ranks),
        out_shape=[jax.ShapeDtypeStruct((2, TILE_ROWS, share * steps), jnp.float32)] * (2 * CHAINS),
        grid_spec=pltpu.PrefetchScalarGridSpec(
            num_scalar_prefetch=4,
            grid=(steps,),
            in_specs=[pl.BlockSpec(memory_space=pl.ANY), integral],
            out_specs=[pl.BlockSpec((2, TILE_ROWS, share), lambda i, *_: (0, 0, i))] * (2 * CHAINS),
            scratch_shapes=[
                pltpu.VMEM((ranks, shards, TILE_ROWS, depth // shards), jnp.float32),
                pltpu.VMEM((rows, 2 * depth), jnp.bfloat16),
                pltpu.VMEM((rows, depth), jnp.bfloat16),
                pltpu.VMEM((rows, COLUMNS), jnp.float32),
                pltpu.SMEM((depth // TILE,), jnp.int32),
                pltpu.SMEM((depth // TILE * ranks,), jnp.int32),
                pltpu.SemaphoreType.DMA((ranks,)),
            ],
        ),
        compiler_params=pltpu.CompilerParams(vmem_limit_bytes=VMEM_BYTES),
        cost_estimate=pl.CostEstimate(
            flops=6 * rows * depth * steps * COLUMNS, bytes_accessed=4 * depth * steps * COLUMNS, transcendentals=0
        ),
    )(source, tile, row_flags, int_tiles, gathered, halves)


def relay_kernel(*refs):
    for chain in range(CHAINS):
        refs[2 * CHAINS + chain][...] = refs[2 * chain][0] + refs[2 * chain + 1][0]


def relay(kept, heard):
    _, rows, width = kept[0].shape
    passed = pl.BlockSpec((1, rows, width), lambda i: (1, 0, 0))
    out = jax.ShapeDtypeStruct((rows, width), jnp.float32)
    return pl.pallas_call(
        relay_kernel,
        out_shape=[out] * CHAINS,
        grid=(1,),
        in_specs=[passed] * (2 * CHAINS),
        out_specs=[pl.BlockSpec((rows, width), lambda i: (0, 0))] * CHAINS,
    )(*[array for pair in zip(kept, heard) for array in pair])


def finish_kernel(columns, *refs):
    refs = refs[1:]
    parts, (term_ref, denominator_ref), out_ref = refs[: 3 * CHAINS], refs[3 * CHAINS : 3 * CHAINS + 2], refs[-1]
    share = columns // CHAINS
    for block in range(term_ref.shape[1] // columns):
        for chain in range(CHAINS):
            kept, heard, relayed = parts[3 * chain : 3 * chain + 3]
            source = pl.ds(block * share, share)
            target = pl.ds(block * columns + chain * share, share)
            total = kept[0, :, source] + heard[0, :, source] + relayed[:, source]
            out_ref[:, target] = (total + term_ref[:, target]) / denominator_ref[:, target]


def finish(r, start, slot, kept, heard, relayed, other_terms, denominators, update):
    blocks = 2 if start == 0 else 1
    share = kept[0].shape[2] // blocks
    width = share * CHAINS
    first = pl.BlockSpec((1, TILE_ROWS, share), lambda i, slot: (0, 0, i))
    whole = pl.BlockSpec((TILE_ROWS, share), lambda i, slot: (0, i))
    owned = pl.BlockSpec((TILE_ROWS, width), lambda i, slot: (slot[r], start * COLUMNS // width + i))
    before = [] if update is None else [update]
    return pl.pallas_call(
        functools.partial(finish_kernel, COLUMNS),
        out_shape=jax.ShapeDtypeStruct(other_terms.shape, jnp.float32),
        grid_spec=pltpu.PrefetchScalarGridSpec(
            num_scalar_prefetch=1,
            grid=(blocks,),
            in_specs=[first, first, whole] * CHAINS
            + [owned, owned]
            + [pl.BlockSpec(memory_space=pl.ANY)] * len(before),
            out_specs=owned,
        ),
        input_output_aliases={3 * CHAINS + 3: 0} if before else {},
        cost_estimate=pl.CostEstimate(flops=0, bytes_accessed=24 * TILE_ROWS * width, transcendentals=0),
    )(
        slot,
        *[array for chain in zip(kept, heard, relayed) for array in chain],
        other_terms,
        denominators,
        *before,
    )


def in_rounds(devices, ranks, amplitudes, amp_tiles, integrals, int_tiles, owner_tiles, other_terms, denominators):
    rank = lax.axis_index("cd").astype(jnp.int32)
    spot = lax.axis_index("ab").astype(jnp.int32)
    tiles = amp_tiles.shape[1]
    half = tiles // CORES

    def gather(array):
        return lax.all_gather(array, "ab", axis=0)

    def swap(sent, peers):
        return [lax.ppermute(array, "cd", [(c, c ^ peer) for c in range(ranks)]) for array, peer in zip(sent, peers)]

    where, source, slot, tile = plan(owner_tiles, jnp.stack([rank, spot]), devices, half)
    whole = take(FIRST, tiles, where, amp_tiles, amplitudes)
    halves = split(integrals)
    away = take(AWAY, half, where, amp_tiles, amplitudes)
    stay = take(STAY, half, where, amp_tiles, amplitudes)
    came = lax.ppermute(away, "ab", [(i, i ^ 1) for i in range(devices)])
    mine = where[WHOSE] == 0
    shards = [whole, jnp.where(mine, stay, came), jnp.where(mine, came, stay)]
    gathered = [gather(shard) for shard in shards]
    terms = (other_terms, denominators)
    tie = lax.optimization_barrier
    steps = halves.shape[1] // COLUMNS
    most = steps * 3 // 4

    def begin(r, rows, first=0, count=steps):
        return product(r, first, count, ranks, source, tile, row_flags, int_tiles, rows, halves)

    def send(parts):
        return swap(parts[1::2], (1, 2))

    def pass_on(parts, heard):
        onward = relay(parts[0::2], heard)
        return onward, swap(onward, (2, 1))

    row_flags, halves = tie((amp_tiles, halves))
    for bit in range((devices - 1).bit_length()):
        reach = 1 << bit
        came = lax.ppermute(row_flags, "ab", [(i, i ^ reach) for i in range(devices)])
        row_flags = jnp.where(
            spot & reach == 0, jnp.concatenate([row_flags, came]), jnp.concatenate([came, row_flags])
        )
    rows, halves, row_flags, *_ = tie((gathered[0], halves, row_flags, *shards[1:]))
    parts0 = begin(0, rows)
    heard0 = send(parts0)
    parts1, heard0 = tie((begin(1, rows), heard0))
    heard1 = send(parts1)
    onward, relayed0 = pass_on(parts0, heard0)

    onward, relayed1 = pass_on(parts1, heard1)
    rows, onward = tie((gathered[1], onward))
    parts2, relayed0, relayed1 = tie((begin(2, rows), relayed0, relayed1))
    parts2, slot, onward = tie((parts2, slot, onward))
    heard2 = send(parts2)
    update = finish(0, 0, slot, parts0[0::2], heard0, relayed0, *terms, None)
    update = finish(1, 0, slot, parts1[0::2], heard1, relayed1, *terms, update)
    heard2, update = tie((heard2, update))
    onward, relayed2 = pass_on(parts2, heard2)

    rows, onward, update = tie((gathered[2], onward, update))
    parts3, relayed2 = tie((begin(3, rows, 0, most), relayed2))
    heard3 = send(parts3)
    parts4, heard3 = tie((begin(3, rows, most, steps - most), heard3))
    heard4 = send(parts4)
    onward, relayed3 = pass_on(parts3, heard3)
    slot, onward = tie((slot, onward))
    update = finish(2, 0, slot, parts2[0::2], heard2, relayed2, *terms, update)
    heard4, update = tie((heard4, update))
    _, relayed4 = pass_on(parts4, heard4)
    update = finish(3, 0, slot, parts3[0::2], heard3, relayed3, *terms, update)
    return finish(3, most, slot, parts4[0::2], heard4, relayed4, *terms, update)


def solution(mesh):
    ranks, places = mesh.shape["cd"], mesh.shape["ab"]

    def on_device(amplitudes, amp_tiles, integrals, int_tiles, owner_tiles, other_terms, denominators):
        args = (amplitudes, amp_tiles, integrals, int_tiles, owner_tiles, other_terms, denominators)
        tiles = owner_tiles.shape[0]
        whole = places % CORES == 0 and amplitudes.shape[1] % (CORES * TILE) == 0
        if whole and ranks == 4 and tiles == 2 * places == ROUNDS * ranks:
            return in_rounds(places, ranks, *args)
        return plain(*args)

    return jax.shard_map(
        on_device,
        mesh=mesh,
        in_specs=(
            P("ab", "cd"),
            P("ab", "cd"),
            P("cd", "ab"),
            P("cd", "ab"),
            P(),
            P("cd", "ab"),
            P("cd", "ab"),
        ),
        out_specs=P("cd", "ab"),
        check_vma=False,
    )
```

profile of v0, /device:TPU:0, one launch (start us, length us, event | category | flops | bytes accessed | tf_op | source)
XLA Modules:
  0.0 413.3 jit_solution(3746362698916555862)
XLA Ops:
  7.1 1.6 shard_map.73
  8.7 4.5 %shard_map.74 = f32[128,4096]{1,0:T(8,128)} custom-call(s32[7]{0:T(128)} %get-tuple-element.87.take_ref, s32[2,4]{1,0:T(2,128)} %flag_ref.10, f32[256,4096]{1,0:T(8,128)} %amp_ref.5), custom_call_target="tpu_custom_call" | custom-call | tf_op jit(solution)/shard_map/pallas_call | solution.py:134
  13.3 2.8 shard_map.77
  16.6 2.8 shard_map.76
  20.6 2.7 broadcast_select_fusion
  24.1 25.0 %shard_map.75.halves_ref = bf16[8192,2048]{1,0:T(8,128)(2,1)} custom-call(f32[4096,2048]{1,0:T(8,128)} %value_ref.1), custom_call_target="tpu_custom_call" | custom-call | bytes 67108864 | tf_op jit(solution)/shard_map/pallas_call | solution.py:157
  49.3 1.1 collective-permute-done
  50.4 4.4 %collective-permute-start.1 = (s32[4,4]{0,1:T(4,128)S(1)}, s32[4,4]{0,1:T(4,128)S(1)}, u32[]{:S(2)}, u32[]{:S(2)}) collective-permute-start(s32[4,4]{0,1:T(4,128)S(1)} %add_select_fusion), channel_id=1, source_target_pairs={{0,2},{1,3},{2,0},{3,1},{4,6},{5,7},{6,4},{7,5},{8,10},{9,11},{10,... | collective-permute-start | bytes 200 | tf_op jit(solution)/shard_map/ppermute | solution.py:368
  54.8 1.6 collective-permute-done.1
  56.5 6.3 %collective-permute-start.2 = (s32[8,4]{0,1:T(4,128)S(1)}, s32[8,4]{0,1:T(4,128)S(1)}, u32[]{:S(2)}, u32[]{:S(2)}) collective-permute-start(s32[8,4]{0,1:T(4,128)S(1)} %add_select_fusion.1), channel_id=1, source_target_pairs={{0,4},{1,5},{2,6},{3,7},{4,0},{5,1},{6,2},{7,3},{8,12},{9,13},{10,... | collective-permute-start | bytes 392 | tf_op jit(solution)/shard_map/ppermute | solution.py:368
  63.4 6.2 %collective-permute-done.2 = s32[8,4]{0,1:T(4,128)S(1)} collective-permute-done((s32[8,4]{0,1:T(4,128)S(1)}, s32[8,4]{0,1:T(4,128)S(1)}, u32[]{:S(2)}, u32[]{:S(2)}) %collective-permute-start.2) | collective-permute-done | bytes 160 | tf_op jit(solution)/shard_map/ppermute | solution.py:368
  70.4 96.8 %all-gather.7.cloned.1.call-done = f32[1024,4096]{1,0:T(8,128)} async-done(((f32[128,4096]{1,0:T(8,128)}), f32[1024,4096]{1,0:T(8,128)}) %all-gather.7.cloned.1.call-update) | async-done | bytes 16777232 | tf_op jit(solution)/shard_map/all_gather | solution.py:336
  167.2 29.4 %shard_map.79 = (f32[2,128,1024]{2,1,0:T(8,128)}, f32[2,128,1024]{2,1,0:T(8,128)}, f32[2,128,1024]{2,1,0:T(8,128)}, f32[2,128,1024]{2,1,0:T(8,128)}) custom-call(s32[16]{0:T(128)} %get-tuple-element.85.source_ref, s32[16]{0:T(128)} %get-tuple-element.86.tile_ref, s32[16,4]{1,0:T(8,128)} %broadcast_select_fusion.2.row_flag_ref, s32[4,2]{1,0:T(4,128)} %copy.24.flag_ref, ...), custom_call_target="tpu_custom_call" | custom-call | flops 25769803776 | bytes 33554432 | tf_op jit(solution)/shard_map/pallas_call | solution.py:243
  196.8 29.6 %shard_map.78 = (f32[2,128,1024]{2,1,0:T(8,128)}, f32[2,128,1024]{2,1,0:T(8,128)}, f32[2,128,1024]{2,1,0:T(8,128)}, f32[2,128,1024]{2,1,0:T(8,128)}) custom-call(s32[16]{0:T(128)} %get-tuple-element.85.source_ref, s32[16]{0:T(128)} %get-tuple-element.86.tile_ref, s32[16,4]{1,0:T(8,128)} %broadcast_select_fusion.2.row_flag_ref, s32[4,2]{1,0:T(4,128)} %copy.24.flag_ref, ...), custom_call_target="tpu_custom_call" | custom-call | flops 25769803776 | bytes 33554432 | tf_op jit(solution)/shard_map/pallas_call | solution.py:243
  226.5 1.9 collective-permute-start.7
  228.4 2.5 shard_map.82
  231.2 1.9 collective-permute-start.9
  233.1 19.7 %collective-permute-done.6.refs_1_.refs_2_ = f32[2,128,1024]{2,1,0:T(8,128)S(1)} collective-permute-done((f32[2,128,1024]{2,1,0:T(8,128)}, f32[2,128,1024]{2,1,0:T(8,128)S(1)}, u32[]{:S(2)}, u32[]{:S(2)}) %collective-permute-start.6) | collective-permute-done | bytes 1048608 | tf_op jit(solution)/shard_map/ppermute | solution.py:339
  252.8 0.9 copy-done.4
  253.8 2.5 shard_map.80
  256.3 1.1 collective-permute-start.11
  257.4 31.3 %shard_map.81 = (f32[2,128,1024]{2,1,0:T(8,128)}, f32[2,128,1024]{2,1,0:T(8,128)}, f32[2,128,1024]{2,1,0:T(8,128)}, f32[2,128,1024]{2,1,0:T(8,128)}) custom-call(s32[16]{0:T(128)} %get-tuple-element.85.source_ref, s32[16]{0:T(128)} %get-tuple-element.86.tile_ref, s32[16,4]{1,0:T(8,128)} %broadcast_select_fusion.2.row_flag_ref, s32[4,2]{1,0:T(4,128)} %copy.24.flag_ref, ...), custom_call_target="tpu_custom_call" | custom-call | flops 25769803776 | bytes 33554432 | tf_op jit(solution)/shard_map/pallas_call | solution.py:243
  288.9 0.7 copy-done.11
  289.8 4.2 %shard_map.83.refs_9_ = f32[512,2048]{1,0:T(8,128)} custom-call(s32[4]{0:T(128)} %get-tuple-element.152.refs_0_, f32[2,128,1024]{2,1,0:T(8,128)} %get-tuple-element.110.refs_0_.refs_1_, f32[2,128,1024]{2,1,0:T(8,128)} %copy-done.2, f32[128,1024]{1,0:T(8,128)} %copy-done.11, f32[2,128,1024]{2,1,0:T(8,128)} %get-tuple-element.112.refs_2_.refs_4_, ...), custom_call_target="tpu_custom_call" | custom-call | bytes 3145728 | tf_op jit(solution)/shard_map/pallas_call | solution.py:307
  294.0 4.2 %shard_map.84.refs_9_ = f32[512,2048]{1,0:T(8,128)} custom-call(s32[4]{0:T(128)} %get-tuple-element.152.refs_0_, f32[2,128,1024]{2,1,0:T(8,128)} %get-tuple-element.99.refs_0_.refs_1_, f32[2,128,1024]{2,1,0:T(8,128)} %copy-done.4, f32[128,1024]{1,0:T(8,128)} %copy-done.13, ...), custom_call_target="tpu_custom_call", output_to_operand_aliasing={{}: (9, {})} | custom-call | bytes 3145728 | tf_op jit(solution)/shard_map/pallas_call | solution.py:307
  298.2 15.9 %collective-permute-done.12.refs_1_.refs_2_ = f32[2,128,1024]{2,1,0:T(8,128)S(1)} collective-permute-done((f32[2,128,1024]{2,1,0:T(8,128)}, f32[2,128,1024]{2,1,0:T(8,128)S(1)}, u32[]{:S(2)}, u32[]{:S(2)}) %collective-permute-start.12) | collective-permute-done | bytes 1048608 | tf_op jit(solution)/shard_map/ppermute | solution.py:339
  314.1 1.1 collective-permute-done.13.refs_3_.refs_5_
  315.2 1.0 copy-done.1
  316.2 2.5 shard_map.85
  318.7 2.0 collective-permute-start.15
  320.8 10.7 %all-gather.11.cloned.1.call-done = f32[1024,2048]{1,0:T(8,128)} async-done(((f32[128,2048]{1,0:T(8,128)}), f32[1024,2048]{1,0:T(8,128)}) %all-gather.11.cloned.1.call-update) | async-done | bytes 8388624 | tf_op jit(solution)/shard_map/all_gather | solution.py:336
  331.4 25.7 %shard_map.86 = (f32[2,128,768]{2,1,0:T(8,128)}, f32[2,128,768]{2,1,0:T(8,128)}, f32[2,128,768]{2,1,0:T(8,128)}, f32[2,128,768]{2,1,0:T(8,128)}) custom-call(s32[16]{0:T(128)} %get-tuple-element.85.source_ref, s32[16]{0:T(128)} %get-tuple-element.86.tile_ref, s32[16,4]{1,0:T(8,128)} %broadcast_select_fusion.2.row_flag_ref, s32[4,2]{1,0:T(4,128)} %copy.24.flag_ref, ...), custom_call_target="tpu_custom_call" | custom-call | flops 19327352832 | bytes 25165824 | tf_op jit(solution)/shard_map/pallas_call | solution.py:243
  357.3 11.7 %shard_map.87 = (f32[2,128,256]{2,1,0:T(8,128)}, f32[2,128,256]{2,1,0:T(8,128)}, f32[2,128,256]{2,1,0:T(8,128)}, f32[2,128,256]{2,1,0:T(8,128)}) custom-call(s32[16]{0:T(128)} %get-tuple-element.85.source_ref, s32[16]{0:T(128)} %get-tuple-element.86.tile_ref, s32[16,4]{1,0:T(8,128)} %broadcast_select_fusion.2.row_flag_ref, s32[4,2]{1,0:T(4,128)} %copy.24.flag_ref, ...), custom_call_target="tpu_custom_call" | custom-call | flops 6442450944 | bytes 8388608 | tf_op jit(solution)/shard_map/pallas_call | solution.py:243
  369.1 4.2 %collective-permute-done.16.refs_1_.refs_2_ = f32[2,128,768]{2,1,0:T(8,128)S(1)} collective-permute-done((f32[2,128,768]{2,1,0:T(8,128)}, f32[2,128,768]{2,1,0:T(8,128)S(1)}, u32[]{:S(2)}, u32[]{:S(2)}) %collective-permute-start.16) | collective-permute-done | bytes 786464 | tf_op jit(solution)/shard_map/ppermute | solution.py:339
  373.3 3.3 collective-permute-done.17.refs_3_.refs_5_
  376.6 3.0 collective-permute-start.18
  379.6 2.3 shard_map.88
  381.9 2.0 collective-permute-start.22
  383.9 4.2 %shard_map.89.refs_9_ = f32[512,2048]{1,0:T(8,128)} custom-call(s32[4]{0:T(128)} %get-tuple-element.152.refs_0_, f32[2,128,1024]{2,1,0:T(8,128)} %get-tuple-element.122.refs_0_.refs_1_, f32[2,128,1024]{2,1,0:T(8,128)} %copy-done, f32[128,1024]{1,0:T(8,128)} %copy-done.9, ...), custom_call_target="tpu_custom_call", output_to_operand_aliasing={{}: (9, {})} | custom-call | bytes 3145728 | tf_op jit(solution)/shard_map/pallas_call | solution.py:307
  388.1 1.0 collective-permute-done.19.refs_3_.refs_5_
  389.1 0.7 copy-done.8
  389.7 1.8 shard_map.90
  392.1 1.2 collective-permute-start.21
  393.3 4.1 collective-permute-done.22.refs_3_
  397.4 0.8 copy-done.15
  398.2 0.8 copy-done.16
  398.9 3.7 shard_map.91.refs_9_
  404.0 2.8 shard_map.92
  (84 shorter events, 6.9 us)
Async XLA Ops:
  6.5 160.7 %all-gather.7.cloned.1.call-start = ((), (), s32[]{:S(2)}) async-start(), calls=%async_computation | async-start | bytes 18874368 | tf_op jit(solution)/shard_map/all_gather | solution.py:336
  13.2 6.1 %copy-start.20 = (s32[7]{0:T(128)S(1)}, s32[7]{0:T(128)}, u32[]{:S(2)}) copy-start(s32[7]{0:T(128)} %get-tuple-element.87.take_ref) | copy-start | bytes 88
  13.2 244.2 %all-gather.9.cloned.1.call-start = ((), (), s32[]{:S(2)}) async-start(), calls=%async_computation.1 | async-start | bytes 9437184 | tf_op jit(solution)/shard_map/all_gather | solution.py:336
  16.1 4.4 %collective-permute-start.3 = (f32[128,2048]{1,0:T(8,128)}, f32[128,2048]{1,0:T(8,128)S(1)}, u32[]{:S(2)}, u32[]{:S(2)}) collective-permute-start(f32[128,2048]{1,0:T(8,128)} %shard_map.77), channel_id=1, source_target_pairs={{0,1},{1,0},{2,3},{3,2},{4,5},{5,4},{6,7},{7,6},{8,9},{9,8},{10,11... | collective-permute-start | bytes 3145736 | tf_op jit(solution)/shard_map/ppermute | solution.py:346
  23.3 308.1 %all-gather.11.cloned.1.call-start = ((), (), s32[]{:S(2)}) async-start(), calls=%async_computation.2 | async-start | bytes 9437184 | tf_op jit(solution)/shard_map/all_gather | solution.py:336
  24.1 25.1 %copy-start.19 = (s32[2,4]{1,0:T(2,128)S(1)}, s32[2,4]{1,0:T(2,128)}, u32[]{:S(2)}) copy-start(s32[2,4]{1,0:T(2,128)} %flag_ref.10) | copy-start | bytes 100
  24.1 38.7 %copy-start.21 = (s32[4,2]{0,1:T(2,128)S(1)}, s32[4,2]{0,1:T(2,128)}, u32[]{:S(2)}) copy-start(s32[4,2]{0,1:T(2,128)} %param.10) | copy-start | bytes 100
  49.2 1.2 collective-permute-start
  50.4 6.0 %collective-permute-start.1 = (s32[4,4]{0,1:T(4,128)S(1)}, s32[4,4]{0,1:T(4,128)S(1)}, u32[]{:S(2)}, u32[]{:S(2)}) collective-permute-start(s32[4,4]{0,1:T(4,128)S(1)} %add_select_fusion), channel_id=1, source_target_pairs={{0,2},{1,3},{2,0},{3,1},{4,6},{5,7},{6,4},{7,5},{8,10},{9,11},{10,... | collective-permute-start | bytes 200 | tf_op jit(solution)/shard_map/ppermute | solution.py:368
  56.5 13.1 %collective-permute-start.2 = (s32[8,4]{0,1:T(4,128)S(1)}, s32[8,4]{0,1:T(4,128)S(1)}, u32[]{:S(2)}, u32[]{:S(2)}) collective-permute-start(s32[8,4]{0,1:T(4,128)S(1)} %add_select_fusion.1), channel_id=1, source_target_pairs={{0,4},{1,5},{2,6},{3,7},{4,0},{5,1},{6,2},{7,3},{8,12},{9,13},{10,... | collective-permute-start | bytes 392 | tf_op jit(solution)/shard_map/ppermute | solution.py:368
  196.7 29.7 %collective-permute-start.4 = (f32[2,128,1024]{2,1,0:T(8,128)}, f32[2,128,1024]{2,1,0:T(8,128)S(1)}, u32[]{:S(2)}, u32[]{:S(2)}) collective-permute-start(f32[2,128,1024]{2,1,0:T(8,128)} %get-tuple-element.97), channel_id=1, source_target_pairs={{0,8},{8,0},{16,24},{24,16},{1,9},{9,1},{17,25},{25,17},{2,10},{10... | collective-permute-start | bytes 3145736 | tf_op jit(solution)/shard_map/ppermute | solution.py:339
  196.8 29.7 %collective-permute-start.5 = (f32[2,128,1024]{2,1,0:T(8,128)}, f32[2,128,1024]{2,1,0:T(8,128)S(1)}, u32[]{:S(2)}, u32[]{:S(2)}) collective-permute-start(f32[2,128,1024]{2,1,0:T(8,128)} %get-tuple-element.98), channel_id=1, source_target_pairs={{0,16},{8,24},{16,0},{24,8},{1,17},{9,25},{17,1},{25,9},{2,18},{10... | collective-permute-start | bytes 3145736 | tf_op jit(solution)/shard_map/ppermute | solution.py:339
  226.4 2.0 copy-start.2
  226.4 2.0 copy-start.3
  226.5 26.4 %collective-permute-start.6 = (f32[2,128,1024]{2,1,0:T(8,128)}, f32[2,128,1024]{2,1,0:T(8,128)S(1)}, u32[]{:S(2)}, u32[]{:S(2)}) collective-permute-start(f32[2,128,1024]{2,1,0:T(8,128)} %get-tuple-element.100), channel_id=1, source_target_pairs={{0,8},{8,0},{16,24},{24,16},{1,9},{9,1},{17,25},{25,17},{2,10},{10... | collective-permute-start | bytes 3145736 | tf_op jit(solution)/shard_map/ppermute | solution.py:339
  226.5 26.3 %collective-permute-start.7 = (f32[2,128,1024]{2,1,0:T(8,128)}, f32[2,128,1024]{2,1,0:T(8,128)}, u32[]{:S(2)}, u32[]{:S(2)}) collective-permute-start(f32[2,128,1024]{2,1,0:T(8,128)} %get-tuple-element.102), channel_id=1, source_target_pairs={{0,16},{8,24},{16,0},{24,8},{1,17},{9,25},{17,1},{25,9},{2,18},{10... | collective-permute-start | bytes 3145736 | tf_op jit(solution)/shard_map/ppermute | solution.py:339
  231.0 57.8 %collective-permute-start.8 = (f32[128,1024]{1,0:T(8,128)}, f32[128,1024]{1,0:T(8,128)S(1)}, u32[]{:S(2)}, u32[]{:S(2)}) collective-permute-start(f32[128,1024]{1,0:T(8,128)} %get-tuple-element.114), channel_id=1, source_target_pairs={{0,16},{8,24},{16,0},{24,8},{1,17},{9,25},{17,1},{25,9},{2,18},{10... | collective-permute-start | bytes 1572872 | tf_op jit(solution)/shard_map/ppermute | solution.py:339
  231.2 57.6 %collective-permute-start.9 = (f32[128,1024]{1,0:T(8,128)}, f32[128,1024]{1,0:T(8,128)S(1)}, u32[]{:S(2)}, u32[]{:S(2)}) collective-permute-start(f32[128,1024]{1,0:T(8,128)} %get-tuple-element.115), channel_id=1, source_target_pairs={{0,8},{8,0},{16,24},{24,16},{1,9},{9,1},{17,25},{25,17},{2,10},{10... | collective-permute-start | bytes 1572872 | tf_op jit(solution)/shard_map/ppermute | solution.py:339
  252.8 1.0 copy-start.4
  256.3 32.5 %collective-permute-start.10 = (f32[128,1024]{1,0:T(8,128)}, f32[128,1024]{1,0:T(8,128)S(1)}, u32[]{:S(2)}, u32[]{:S(2)}) collective-permute-start(f32[128,1024]{1,0:T(8,128)} %get-tuple-element.103), channel_id=1, source_target_pairs={{0,16},{8,24},{16,0},{24,8},{1,17},{9,25},{17,1},{25,9},{2,18},{10... | collective-permute-start | bytes 1572872 | tf_op jit(solution)/shard_map/ppermute | solution.py:339
  256.3 32.5 %collective-permute-start.11 = (f32[128,1024]{1,0:T(8,128)}, f32[128,1024]{1,0:T(8,128)S(1)}, u32[]{:S(2)}, u32[]{:S(2)}) collective-permute-start(f32[128,1024]{1,0:T(8,128)} %get-tuple-element.104), channel_id=1, source_target_pairs={{0,8},{8,0},{16,24},{24,16},{1,9},{9,1},{17,25},{25,17},{2,10},{10... | collective-permute-start | bytes 1572872 | tf_op jit(solution)/shard_map/ppermute | solution.py:339
  288.8 0.8 copy-start.11
  288.8 1.0 copy-start.12
  288.8 5.2 %copy-start.13 = (f32[128,1024]{1,0:T(8,128)}, f32[128,1024]{1,0:T(8,128)S(1)}, u32[]{:S(2)}) copy-start(f32[128,1024]{1,0:T(8,128)S(1)} %collective-permute-done.10.refs_3_) | copy-start | bytes 1572868
  288.9 5.2 %copy-start.14 = (f32[128,1024]{1,0:T(8,128)}, f32[128,1024]{1,0:T(8,128)S(1)}, u32[]{:S(2)}) copy-start(f32[128,1024]{1,0:T(8,128)S(1)} %collective-permute-done.11.refs_6_) | copy-start | bytes 1572868
  289.8 24.3 %collective-permute-start.12 = (f32[2,128,1024]{2,1,0:T(8,128)}, f32[2,128,1024]{2,1,0:T(8,128)S(1)}, u32[]{:S(2)}, u32[]{:S(2)}) collective-permute-start(f32[2,128,1024]{2,1,0:T(8,128)} %get-tuple-element.123), channel_id=1, source_target_pairs={{0,8},{8,0},{16,24},{24,16},{1,9},{9,1},{17,25},{25,17},{2,10},{10... | collective-permute-start | bytes 3145736 | tf_op jit(solution)/shard_map/ppermute | solution.py:339
  289.8 25.4 %collective-permute-start.13 = (f32[2,128,1024]{2,1,0:T(8,128)}, f32[2,128,1024]{2,1,0:T(8,128)S(1)}, u32[]{:S(2)}, u32[]{:S(2)}) collective-permute-start(f32[2,128,1024]{2,1,0:T(8,128)} %get-tuple-element.124), channel_id=1, source_target_pairs={{0,16},{8,24},{16,0},{24,8},{1,17},{9,25},{17,1},{25,9},{2,18},{10... | collective-permute-start | bytes 3145736 | tf_op jit(solution)/shard_map/ppermute | solution.py:339
  314.1 1.1 copy-start
  315.2 1.0 copy-start.1
  318.7 38.4 %collective-permute-start.14 = (f32[128,1024]{1,0:T(8,128)}, f32[128,1024]{1,0:T(8,128)S(1)}, u32[]{:S(2)}, u32[]{:S(2)}) collective-permute-start(f32[128,1024]{1,0:T(8,128)} %get-tuple-element.132), channel_id=1, source_target_pairs={{0,16},{8,24},{16,0},{24,8},{1,17},{9,25},{17,1},{25,9},{2,18},{10... | collective-permute-start | bytes 1572872 | tf_op jit(solution)/shard_map/ppermute | solution.py:339
  318.7 38.4 %collective-permute-start.15 = (f32[128,1024]{1,0:T(8,128)}, f32[128,1024]{1,0:T(8,128)S(1)}, u32[]{:S(2)}, u32[]{:S(2)}) collective-permute-start(f32[128,1024]{1,0:T(8,128)} %get-tuple-element.133), channel_id=1, source_target_pairs={{0,8},{8,0},{16,24},{24,16},{1,9},{9,1},{17,25},{25,17},{2,10},{10... | collective-permute-start | bytes 1572872 | tf_op jit(solution)/shard_map/ppermute | solution.py:339
  357.1 11.9 %copy-start.9 = (f32[128,1024]{1,0:T(8,128)}, f32[128,1024]{1,0:T(8,128)S(1)}, u32[]{:S(2)}) copy-start(f32[128,1024]{1,0:T(8,128)S(1)} %collective-permute-done.14.refs_3_) | copy-start | bytes 1572868
  357.2 11.9 %copy-start.10 = (f32[128,1024]{1,0:T(8,128)}, f32[128,1024]{1,0:T(8,128)S(1)}, u32[]{:S(2)}) copy-start(f32[128,1024]{1,0:T(8,128)S(1)} %collective-permute-done.15.refs_6_) | copy-start | bytes 1572868
  357.2 16.1 %collective-permute-start.16 = (f32[2,128,768]{2,1,0:T(8,128)}, f32[2,128,768]{2,1,0:T(8,128)S(1)}, u32[]{:S(2)}, u32[]{:S(2)}) collective-permute-start(f32[2,128,768]{2,1,0:T(8,128)} %get-tuple-element.145), channel_id=1, source_target_pairs={{0,8},{8,0},{16,24},{24,16},{1,9},{9,1},{17,25},{25,17},{2,10},{10... | collective-permute-start | bytes 2359304 | tf_op jit(solution)/shard_map/ppermute | solution.py:339
  357.3 19.3 %collective-permute-start.17 = (f32[2,128,768]{2,1,0:T(8,128)}, f32[2,128,768]{2,1,0:T(8,128)S(1)}, u32[]{:S(2)}, u32[]{:S(2)}) collective-permute-start(f32[2,128,768]{2,1,0:T(8,128)} %get-tuple-element.146), channel_id=1, source_target_pairs={{0,16},{8,24},{16,0},{24,8},{1,17},{9,25},{17,1},{25,9},{2,18},{10... | collective-permute-start | bytes 2359304 | tf_op jit(solution)/shard_map/ppermute | solution.py:339
  373.3 6.4 %copy-start.5 = (f32[2,128,768]{2,1,0:T(8,128)}, f32[2,128,768]{2,1,0:T(8,128)S(1)}, u32[]{:S(2)}) copy-start(f32[2,128,768]{2,1,0:T(8,128)S(1)} %collective-permute-done.16.refs_1_.refs_2_) | copy-start | bytes 2359300
  376.6 3.0 copy-start.6
  376.6 11.5 %collective-permute-start.18 = (f32[2,128,256]{2,1,0:T(8,128)}, f32[2,128,256]{2,1,0:T(8,128)S(1)}, u32[]{:S(2)}, u32[]{:S(2)}) collective-permute-start(f32[2,128,256]{2,1,0:T(8,128)} %get-tuple-element.154), channel_id=1, source_target_pairs={{0,8},{8,0},{16,24},{24,16},{1,9},{9,1},{17,25},{25,17},{2,10},{10... | collective-permute-start | bytes 786440 | tf_op jit(solution)/shard_map/ppermute | solution.py:339
  379.6 9.4 %collective-permute-start.19 = (f32[2,128,256]{2,1,0:T(8,128)}, f32[2,128,256]{2,1,0:T(8,128)S(1)}, u32[]{:S(2)}, u32[]{:S(2)}) collective-permute-start(f32[2,128,256]{2,1,0:T(8,128)} %get-tuple-element.155), channel_id=1, source_target_pairs={{0,16},{8,24},{16,0},{24,8},{1,17},{9,25},{17,1},{25,9},{2,18},{10... | collective-permute-start | bytes 786440 | tf_op jit(solution)/shard_map/ppermute | solution.py:339
  381.9 15.5 %collective-permute-start.22 = (f32[128,768]{1,0:T(8,128)}, f32[128,768]{1,0:T(8,128)S(1)}, u32[]{:S(2)}, u32[]{:S(2)}) collective-permute-start(f32[128,768]{1,0:T(8,128)} %get-tuple-element.150), channel_id=1, source_target_pairs={{0,16},{8,24},{16,0},{24,8},{1,17},{9,25},{17,1},{25,9},{2,18},{10... | collective-permute-start | bytes 1179656 | tf_op jit(solution)/shard_map/ppermute | solution.py:339
  383.9 13.5 %collective-permute-start.23 = (f32[128,768]{1,0:T(8,128)}, f32[128,768]{1,0:T(8,128)S(1)}, u32[]{:S(2)}, u32[]{:S(2)}) collective-permute-start(f32[128,768]{1,0:T(8,128)} %get-tuple-element.151), channel_id=1, source_target_pairs={{0,8},{8,0},{16,24},{24,16},{1,9},{9,1},{17,25},{25,17},{2,10},{10... | collective-permute-start | bytes 1179656 | tf_op jit(solution)/shard_map/ppermute | solution.py:339
  388.1 1.0 copy-start.7
  389.1 0.7 copy-start.8
  391.6 11.1 %collective-permute-start.20 = (f32[128,256]{1,0:T(8,128)}, f32[128,256]{1,0:T(8,128)S(1)}, u32[]{:S(2)}, u32[]{:S(2)}) collective-permute-start(f32[128,256]{1,0:T(8,128)} %get-tuple-element.162), channel_id=1, source_target_pairs={{0,16},{8,24},{16,0},{24,8},{1,17},{9,25},{17,1},{25,9},{2,18},{10... | collective-permute-start | bytes 393224 | tf_op jit(solution)/shard_map/ppermute | solution.py:339
  392.1 10.5 %collective-permute-start.21 = (f32[128,256]{1,0:T(8,128)}, f32[128,256]{1,0:T(8,128)S(1)}, u32[]{:S(2)}, u32[]{:S(2)}) collective-permute-start(f32[128,256]{1,0:T(8,128)} %get-tuple-element.163), channel_id=1, source_target_pairs={{0,8},{8,0},{16,24},{24,16},{1,9},{9,1},{17,25},{25,17},{2,10},{10... | collective-permute-start | bytes 393224 | tf_op jit(solution)/shard_map/ppermute | solution.py:339
  397.4 0.8 copy-start.15
  398.2 0.8 copy-start.16
  403.3 0.6 copy-start.18
  (1 other events, 0.6 us)
Sparse Core Ops, SparseCore 0:
  13.3 153.8 all-gather.6
  168.8 80.3 all-gather.8
  250.8 80.5 all-gather.10
where the time goes:
time: 412 us; the launch traced here: 413 us
  Pallas kernels  195 us (47%)
  waiting for transfers between devices  166 us (40%)
  starting transfers between devices  25.6 us (6%)
  between operations  14.1 us (3%)
  local copies, waits for them, and re-layouts  7.92 us (2%)
    pallas_call x5, Pallas kernels, product(): pl.pallas_call(functools.partial(product_kernel, r, first, ranks), out_sh...  128 us
    all_gather x3, waiting for transfers between devices, gather(): return lax.all_gather(array, 'ab', axis=0)  107 us
    ppermute x20, waiting for transfers between devices, swap(): lax.ppermute(array, 'cd', [(c, c ^ peer) for c in range(ranks)])  49.3 us
    pallas_call x1, Pallas kernels, split(): pl.pallas_call(split_kernel, out_shape=jax.ShapeDtypeStruct((2 * depth, w...  25 us
    pallas_call x5, Pallas kernels, finish(): pl.pallas_call(functools.partial(finish_kernel, COLUMNS), out_shape=jax.S...  19.1 us
    ppermute x20, starting transfers between devices, swap(): lax.ppermute(array, 'cd', [(c, c ^ peer) for c in range(ranks)])  14.3 us
    pallas_call x5, Pallas kernels, relay(): pl.pallas_call(relay_kernel, out_shape=[out] * CHAINS, grid=(1,), in_spec...  11.7 us
    ppermute x3, starting transfers between devices, in_rounds(): lax.ppermute(row_flags, 'ab', [(i, i ^ reach) for i in range(devices)])  10.7 us
  transfers between devices with their start and end apart: 27, of which 12 were waited for; matrix products, arithmetic and copies ran while one was open for 1% of the time, Pallas kernels for 45%

commit v1 on v0

--- a/solution.py
+++ b/solution.py
@@ -392,10 +392,9 @@
     parts4, heard3 = tie((begin(3, rows, most, steps - most), heard3))
     heard4 = send(parts4)
     onward, relayed3 = pass_on(parts3, heard3)
+    onward, relayed4 = pass_on(parts4, heard4)
     slot, onward = tie((slot, onward))
     update = finish(2, 0, slot, parts2[0::2], heard2, relayed2, *terms, update)
-    heard4, update = tie((heard4, update))
-    _, relayed4 = pass_on(parts4, heard4)
     update = finish(3, 0, slot, parts3[0::2], heard3, relayed3, *terms, update)
     return finish(3, most, slot, parts4[0::2], heard4, relayed4, *terms, update)
 

time: 412 us -> 415 us (level)
  starting transfers between devices: 25.6 us -> 44.6 us
  Pallas kernels: 195 us -> 180 us
    ppermute x20, starting transfers between devices: 14.3 us -> 33.3 us  [swap(): lax.ppermute(array, 'cd', [(c, c ^ peer) for c in range(ranks)])]
    pallas_call x5, Pallas kernels: 128 us -> 112 us  [product(): pl.pallas_call(functools.partial(product_kernel, r, first, ranks), out_sh...]
  transfers between devices with their start and end apart: 27 -> 27, of which waited for: 12 -> 12; matrix products, arithmetic and copies ran while one was open for 1% -> 1% of each run, Pallas kernels for 45% -> 41%
where the time goes in v1:
time: 415 us; the launch traced here: 413 us
  Pallas kernels  180 us (43%)
  waiting for transfers between devices  162 us (39%)
  starting transfers between devices  44.6 us (11%)
  between operations  14.1 us (3%)
  local copies, waits for them, and re-layouts  8.5 us (2%)
    pallas_call x5, Pallas kernels, product(): pl.pallas_call(functools.partial(product_kernel, r, first, ranks), out_sh...  112 us
    all_gather x3, waiting for transfers between devices, gather(): return lax.all_gather(array, 'ab', axis=0)  105 us
    ppermute x20, waiting for transfers between devices, swap(): lax.ppermute(array, 'cd', [(c, c ^ peer) for c in range(ranks)])  47.6 us
    ppermute x20, starting transfers between devices, swap(): lax.ppermute(array, 'cd', [(c, c ^ peer) for c in range(ranks)])  33.3 us
    pallas_call x1, Pallas kernels, split(): pl.pallas_call(split_kernel, out_shape=jax.ShapeDtypeStruct((2 * depth, w...  25 us
    pallas_call x5, Pallas kernels, finish(): pl.pallas_call(functools.partial(finish_kernel, COLUMNS), out_shape=jax.S...  19 us
    pallas_call x5, Pallas kernels, relay(): pl.pallas_call(relay_kernel, out_shape=[out] * CHAINS, grid=(1,), in_spec...  11.9 us
    ppermute x3, starting transfers between devices, in_rounds(): lax.ppermute(row_flags, 'ab', [(i, i ^ reach) for i in range(devices)])  10.7 us
  transfers between devices with their start and end apart: 27, of which 12 were waited for; matrix products, arithmetic and copies ran while one was open for 1% of the time, Pallas kernels for 41%

profile of v1, /device:TPU:0, one launch (start us, length us, event | category | flops | bytes accessed | tf_op | source)
XLA Modules:
  0.0 412.9 jit_solution(10598321748475964106)
XLA Ops:
  7.1 1.6 shard_map.73
  8.7 4.5 %shard_map.74 = f32[128,4096]{1,0:T(8,128)} custom-call(s32[7]{0:T(128)} %get-tuple-element.84.take_ref, s32[2,4]{1,0:T(2,128)} %flag_ref.10, f32[256,4096]{1,0:T(8,128)} %amp_ref.5), custom_call_target="tpu_custom_call" | custom-call | tf_op jit(solution)/shard_map/pallas_call | solution.py:134
  13.3 2.8 shard_map.77
  16.5 2.8 shard_map.76
  20.5 2.7 broadcast_select_fusion
  24.1 25.0 %shard_map.75.halves_ref = bf16[8192,2048]{1,0:T(8,128)(2,1)} custom-call(f32[4096,2048]{1,0:T(8,128)} %value_ref.1), custom_call_target="tpu_custom_call" | custom-call | bytes 67108864 | tf_op jit(solution)/shard_map/pallas_call | solution.py:157
  49.3 1.1 collective-permute-done
  50.4 4.4 %collective-permute-start.1 = (s32[4,4]{0,1:T(4,128)S(1)}, s32[4,4]{0,1:T(4,128)S(1)}, u32[]{:S(2)}, u32[]{:S(2)}) collective-permute-start(s32[4,4]{0,1:T(4,128)S(1)} %add_select_fusion), channel_id=1, source_target_pairs={{0,2},{1,3},{2,0},{3,1},{4,6},{5,7},{6,4},{7,5},{8,10},{9,11},{10,... | collective-permute-start | bytes 200 | tf_op jit(solution)/shard_map/ppermute | solution.py:368
  54.8 1.6 collective-permute-done.1
  56.5 6.3 %collective-permute-start.2 = (s32[8,4]{0,1:T(4,128)S(1)}, s32[8,4]{0,1:T(4,128)S(1)}, u32[]{:S(2)}, u32[]{:S(2)}) collective-permute-start(s32[8,4]{0,1:T(4,128)S(1)} %add_select_fusion.1), channel_id=1, source_target_pairs={{0,4},{1,5},{2,6},{3,7},{4,0},{5,1},{6,2},{7,3},{8,12},{9,13},{10,... | collective-permute-start | bytes 392 | tf_op jit(solution)/shard_map/ppermute | solution.py:368
  63.4 6.2 %collective-permute-done.2 = s32[8,4]{0,1:T(4,128)S(1)} collective-permute-done((s32[8,4]{0,1:T(4,128)S(1)}, s32[8,4]{0,1:T(4,128)S(1)}, u32[]{:S(2)}, u32[]{:S(2)}) %collective-permute-start.2) | collective-permute-done | bytes 160 | tf_op jit(solution)/shard_map/ppermute | solution.py:368
  70.4 96.8 %all-gather.7.cloned.1.call-done = f32[1024,4096]{1,0:T(8,128)} async-done(((f32[128,4096]{1,0:T(8,128)}), f32[1024,4096]{1,0:T(8,128)}) %all-gather.7.cloned.1.call-update) | async-done | bytes 16777232 | tf_op jit(solution)/shard_map/all_gather | solution.py:336
  167.2 27.1 %shard_map.79 = (f32[2,128,1024]{2,1,0:T(8,128)}, f32[2,128,1024]{2,1,0:T(8,128)}, f32[2,128,1024]{2,1,0:T(8,128)}, f32[2,128,1024]{2,1,0:T(8,128)}) custom-call(s32[16]{0:T(128)} %get-tuple-element.82.source_ref, s32[16]{0:T(128)} %get-tuple-element.83.tile_ref, s32[16,4]{1,0:T(8,128)} %broadcast_select_fusion.2.row_flag_ref, s32[4,2]{1,0:T(4,128)} %copy.24.flag_ref, ...), custom_call_target="tpu_custom_call" | custom-call | flops 25769803776 | bytes 33554432 | tf_op jit(solution)/shard_map/pallas_call | solution.py:243
  194.4 3.8 collective-permute-start.4
  198.2 2.2 collective-permute-start.5
  200.3 25.4 %shard_map.78 = (f32[2,128,1024]{2,1,0:T(8,128)}, f32[2,128,1024]{2,1,0:T(8,128)}, f32[2,128,1024]{2,1,0:T(8,128)}, f32[2,128,1024]{2,1,0:T(8,128)}) custom-call(s32[16]{0:T(128)} %get-tuple-element.82.source_ref, s32[16]{0:T(128)} %get-tuple-element.83.tile_ref, s32[16,4]{1,0:T(8,128)} %broadcast_select_fusion.2.row_flag_ref, s32[4,2]{1,0:T(4,128)} %copy.24.flag_ref, ...), custom_call_target="tpu_custom_call" | custom-call | flops 25769803776 | bytes 33554432 | tf_op jit(solution)/shard_map/pallas_call | solution.py:243
  225.8 4.5 %collective-permute-start.6 = (f32[2,128,1024]{2,1,0:T(8,128)}, f32[2,128,1024]{2,1,0:T(8,128)S(1)}, u32[]{:S(2)}, u32[]{:S(2)}) collective-permute-start(f32[2,128,1024]{2,1,0:T(8,128)} %get-tuple-element.97), channel_id=1, source_target_pairs={{0,8},{8,0},{16,24},{24,16},{1,9},{9,1},{17,25},{25,17},{2,10},{10... | collective-permute-start | bytes 3145736 | tf_op jit(solution)/shard_map/ppermute | solution.py:339
  230.3 2.5 shard_map.82
  232.9 2.1 collective-permute-start.8
  235.0 19.5 %collective-permute-done.6.refs_1_.refs_2_ = f32[2,128,1024]{2,1,0:T(8,128)S(1)} collective-permute-done((f32[2,128,1024]{2,1,0:T(8,128)}, f32[2,128,1024]{2,1,0:T(8,128)S(1)}, u32[]{:S(2)}, u32[]{:S(2)}) %collective-permute-start.6) | collective-permute-done | bytes 1048608 | tf_op jit(solution)/shard_map/ppermute | solution.py:339
  254.5 2.1 collective-permute-done.7.refs_3_.refs_5_
  256.7 2.7 shard_map.80
  259.4 0.9 collective-permute-start.11
  260.3 25.2 %shard_map.81 = (f32[2,128,1024]{2,1,0:T(8,128)}, f32[2,128,1024]{2,1,0:T(8,128)}, f32[2,128,1024]{2,1,0:T(8,128)}, f32[2,128,1024]{2,1,0:T(8,128)}) custom-call(s32[16]{0:T(128)} %get-tuple-element.82.source_ref, s32[16]{0:T(128)} %get-tuple-element.83.tile_ref, s32[16,4]{1,0:T(8,128)} %broadcast_select_fusion.2.row_flag_ref, s32[4,2]{1,0:T(4,128)} %copy.24.flag_ref, ...), custom_call_target="tpu_custom_call" | custom-call | flops 25769803776 | bytes 33554432 | tf_op jit(solution)/shard_map/pallas_call | solution.py:243
  286.6 7.0 %collective-permute-start.12 = (f32[2,128,1024]{2,1,0:T(8,128)}, f32[2,128,1024]{2,1,0:T(8,128)S(1)}, u32[]{:S(2)}, u32[]{:S(2)}) collective-permute-start(f32[2,128,1024]{2,1,0:T(8,128)} %get-tuple-element.120), channel_id=1, source_target_pairs={{0,8},{8,0},{16,24},{24,16},{1,9},{9,1},{17,25},{25,17},{2,10},{10... | collective-permute-start | bytes 3145736 | tf_op jit(solution)/shard_map/ppermute | solution.py:339
  293.6 4.2 %shard_map.83.refs_9_ = f32[512,2048]{1,0:T(8,128)} custom-call(s32[4]{0:T(128)} %get-tuple-element.149.refs_0_, f32[2,128,1024]{2,1,0:T(8,128)} %get-tuple-element.107.refs_0_.refs_1_, f32[2,128,1024]{2,1,0:T(8,128)} %copy-done.2, f32[128,1024]{1,0:T(8,128)} %copy-done.11, f32[2,128,1024]{2,1,0:T(8,128)} %get-tuple-element.109.refs_2_.refs_4_, ...), custom_call_target="tpu_custom_call" | custom-call | bytes 3145728 | tf_op jit(solution)/shard_map/pallas_call | solution.py:307
  297.8 4.2 %shard_map.84.refs_9_ = f32[512,2048]{1,0:T(8,128)} custom-call(s32[4]{0:T(128)} %get-tuple-element.149.refs_0_, f32[2,128,1024]{2,1,0:T(8,128)} %get-tuple-element.96.refs_0_.refs_1_, f32[2,128,1024]{2,1,0:T(8,128)} %copy-done.4, f32[128,1024]{1,0:T(8,128)} %copy-done.13, ...), custom_call_target="tpu_custom_call", output_to_operand_aliasing={{}: (9, {})} | custom-call | bytes 3145728 | tf_op jit(solution)/shard_map/pallas_call | solution.py:307
  302.0 15.7 %collective-permute-done.12.refs_1_.refs_2_ = f32[2,128,1024]{2,1,0:T(8,128)S(1)} collective-permute-done((f32[2,128,1024]{2,1,0:T(8,128)}, f32[2,128,1024]{2,1,0:T(8,128)S(1)}, u32[]{:S(2)}, u32[]{:S(2)}) %collective-permute-start.12) | collective-permute-done | bytes 1048608 | tf_op jit(solution)/shard_map/ppermute | solution.py:339
  317.6 1.1 collective-permute-done.13.refs_3_.refs_5_
  318.7 1.0 copy-done.1
  319.7 2.5 shard_map.85
  322.5 1.0 collective-permute-start.15
  323.5 7.9 %all-gather.11.cloned.1.call-done = f32[1024,2048]{1,0:T(8,128)} async-done(((f32[128,2048]{1,0:T(8,128)}), f32[1024,2048]{1,0:T(8,128)}) %all-gather.11.cloned.1.call-update) | async-done | bytes 8388624 | tf_op jit(solution)/shard_map/all_gather | solution.py:336
  331.4 20.7 %shard_map.87 = (f32[2,128,768]{2,1,0:T(8,128)}, f32[2,128,768]{2,1,0:T(8,128)}, f32[2,128,768]{2,1,0:T(8,128)}, f32[2,128,768]{2,1,0:T(8,128)}) custom-call(s32[16]{0:T(128)} %get-tuple-element.82.source_ref, s32[16]{0:T(128)} %get-tuple-element.83.tile_ref, s32[16,4]{1,0:T(8,128)} %broadcast_select_fusion.2.row_flag_ref, s32[4,2]{1,0:T(4,128)} %copy.24.flag_ref, ...), custom_call_target="tpu_custom_call" | custom-call | flops 19327352832 | bytes 25165824 | tf_op jit(solution)/shard_map/pallas_call | solution.py:243
  352.2 7.0 %collective-permute-start.16 = (f32[2,128,768]{2,1,0:T(8,128)}, f32[2,128,768]{2,1,0:T(8,128)S(1)}, u32[]{:S(2)}, u32[]{:S(2)}) collective-permute-start(f32[2,128,768]{2,1,0:T(8,128)} %get-tuple-element.141), channel_id=1, source_target_pairs={{0,8},{8,0},{16,24},{24,16},{1,9},{9,1},{17,25},{25,17},{2,10},{10... | collective-permute-start | bytes 2359304 | tf_op jit(solution)/shard_map/ppermute | solution.py:339
  359.2 13.7 %shard_map.86 = (f32[2,128,256]{2,1,0:T(8,128)}, f32[2,128,256]{2,1,0:T(8,128)}, f32[2,128,256]{2,1,0:T(8,128)}, f32[2,128,256]{2,1,0:T(8,128)}) custom-call(s32[16]{0:T(128)} %get-tuple-element.82.source_ref, s32[16]{0:T(128)} %get-tuple-element.83.tile_ref, s32[16,4]{1,0:T(8,128)} %broadcast_select_fusion.2.row_flag_ref, s32[4,2]{1,0:T(4,128)} %copy.24.flag_ref, ...), custom_call_target="tpu_custom_call" | custom-call | flops 6442450944 | bytes 8388608 | tf_op jit(solution)/shard_map/pallas_call | solution.py:243
  372.9 3.4 collective-permute-done.16.refs_1_.refs_2_
  376.3 2.6 collective-permute-done.17.refs_3_.refs_5_
  378.9 0.9 copy-done.6
  379.8 2.3 shard_map.89
  382.1 1.2 collective-permute-start.22
  383.2 2.0 collective-permute-start.23
  385.2 3.1 collective-permute-done.18.refs_1_.refs_2_
  389.7 1.8 shard_map.88
  391.5 1.3 collective-permute-start.21
  392.9 4.2 %shard_map.90.refs_9_ = f32[512,2048]{1,0:T(8,128)} custom-call(s32[4]{0:T(128)} %get-tuple-element.149.refs_0_, f32[2,128,1024]{2,1,0:T(8,128)} %get-tuple-element.119.refs_0_.refs_1_, f32[2,128,1024]{2,1,0:T(8,128)} %copy-done, f32[128,1024]{1,0:T(8,128)} %copy-done.9, ...), custom_call_target="tpu_custom_call", output_to_operand_aliasing={{}: (9, {})} | custom-call | bytes 3145728 | tf_op jit(solution)/shard_map/pallas_call | solution.py:307
  398.5 3.7 shard_map.91.refs_9_
  403.5 2.8 shard_map.92
  (84 shorter events, 9.7 us)
Async XLA Ops:
  6.5 160.7 %all-gather.7.cloned.1.call-start = ((), (), s32[]{:S(2)}) async-start(), calls=%async_computation | async-start | bytes 18874368 | tf_op jit(solution)/shard_map/all_gather | solution.py:336
  13.2 6.1 %copy-start.20 = (s32[7]{0:T(128)S(1)}, s32[7]{0:T(128)}, u32[]{:S(2)}) copy-start(s32[7]{0:T(128)} %get-tuple-element.84.take_ref) | copy-start | bytes 88
  13.2 247.1 %all-gather.9.cloned.1.call-start = ((), (), s32[]{:S(2)}) async-start(), calls=%async_computation.1 | async-start | bytes 9437184 | tf_op jit(solution)/shard_map/all_gather | solution.py:336
  16.1 4.4 %collective-permute-start.3 = (f32[128,2048]{1,0:T(8,128)}, f32[128,2048]{1,0:T(8,128)S(1)}, u32[]{:S(2)}, u32[]{:S(2)}) collective-permute-start(f32[128,2048]{1,0:T(8,128)} %shard_map.77), channel_id=1, source_target_pairs={{0,1},{1,0},{2,3},{3,2},{4,5},{5,4},{6,7},{7,6},{8,9},{9,8},{10,11... | collective-permute-start | bytes 3145736 | tf_op jit(solution)/shard_map/ppermute | solution.py:346
  23.3 308.1 %all-gather.11.cloned.1.call-start = ((), (), s32[]{:S(2)}) async-start(), calls=%async_computation.2 | async-start | bytes 9437184 | tf_op jit(solution)/shard_map/all_gather | solution.py:336
  24.0 25.1 %copy-start.19 = (s32[2,4]{1,0:T(2,128)S(1)}, s32[2,4]{1,0:T(2,128)}, u32[]{:S(2)}) copy-start(s32[2,4]{1,0:T(2,128)} %flag_ref.10) | copy-start | bytes 100
  24.1 38.7 %copy-start.21 = (s32[4,2]{0,1:T(2,128)S(1)}, s32[4,2]{0,1:T(2,128)}, u32[]{:S(2)}) copy-start(s32[4,2]{0,1:T(2,128)} %param.10) | copy-start | bytes 100
  49.2 1.2 collective-permute-start
  50.4 6.0 %collective-permute-start.1 = (s32[4,4]{0,1:T(4,128)S(1)}, s32[4,4]{0,1:T(4,128)S(1)}, u32[]{:S(2)}, u32[]{:S(2)}) collective-permute-start(s32[4,4]{0,1:T(4,128)S(1)} %add_select_fusion), channel_id=1, source_target_pairs={{0,2},{1,3},{2,0},{3,1},{4,6},{5,7},{6,4},{7,5},{8,10},{9,11},{10,... | collective-permute-start | bytes 200 | tf_op jit(solution)/shard_map/ppermute | solution.py:368
  56.5 13.1 %collective-permute-start.2 = (s32[8,4]{0,1:T(4,128)S(1)}, s32[8,4]{0,1:T(4,128)S(1)}, u32[]{:S(2)}, u32[]{:S(2)}) collective-permute-start(s32[8,4]{0,1:T(4,128)S(1)} %add_select_fusion.1), channel_id=1, source_target_pairs={{0,4},{1,5},{2,6},{3,7},{4,0},{5,1},{6,2},{7,3},{8,12},{9,13},{10,... | collective-permute-start | bytes 392 | tf_op jit(solution)/shard_map/ppermute | solution.py:368
  194.4 31.4 %collective-permute-start.4 = (f32[2,128,1024]{2,1,0:T(8,128)}, f32[2,128,1024]{2,1,0:T(8,128)S(1)}, u32[]{:S(2)}, u32[]{:S(2)}) collective-permute-start(f32[2,128,1024]{2,1,0:T(8,128)} %get-tuple-element.94), channel_id=1, source_target_pairs={{0,8},{8,0},{16,24},{24,16},{1,9},{9,1},{17,25},{25,17},{2,10},{10... | collective-permute-start | bytes 3145736 | tf_op jit(solution)/shard_map/ppermute | solution.py:339
  198.2 27.6 %collective-permute-start.5 = (f32[2,128,1024]{2,1,0:T(8,128)}, f32[2,128,1024]{2,1,0:T(8,128)S(1)}, u32[]{:S(2)}, u32[]{:S(2)}) collective-permute-start(f32[2,128,1024]{2,1,0:T(8,128)} %get-tuple-element.95), channel_id=1, source_target_pairs={{0,16},{8,24},{16,0},{24,8},{1,17},{9,25},{17,1},{25,9},{2,18},{10... | collective-permute-start | bytes 3145736 | tf_op jit(solution)/shard_map/ppermute | solution.py:339
  225.8 4.6 %copy-start.2 = (f32[2,128,1024]{2,1,0:T(8,128)}, f32[2,128,1024]{2,1,0:T(8,128)S(1)}, u32[]{:S(2)}) copy-start(f32[2,128,1024]{2,1,0:T(8,128)S(1)} %collective-permute-done.4.refs_1_.refs_2_) | copy-start | bytes 3145732
  225.8 4.6 %copy-start.3 = (f32[2,128,1024]{2,1,0:T(8,128)}, f32[2,128,1024]{2,1,0:T(8,128)S(1)}, u32[]{:S(2)}) copy-start(f32[2,128,1024]{2,1,0:T(8,128)S(1)} %collective-permute-done.5.refs_3_.refs_5_) | copy-start | bytes 3145732
  225.8 28.7 %collective-permute-start.6 = (f32[2,128,1024]{2,1,0:T(8,128)}, f32[2,128,1024]{2,1,0:T(8,128)S(1)}, u32[]{:S(2)}, u32[]{:S(2)}) collective-permute-start(f32[2,128,1024]{2,1,0:T(8,128)} %get-tuple-element.97), channel_id=1, source_target_pairs={{0,8},{8,0},{16,24},{24,16},{1,9},{9,1},{17,25},{25,17},{2,10},{10... | collective-permute-start | bytes 3145736 | tf_op jit(solution)/shard_map/ppermute | solution.py:339
  230.3 26.3 %collective-permute-start.7 = (f32[2,128,1024]{2,1,0:T(8,128)}, f32[2,128,1024]{2,1,0:T(8,128)}, u32[]{:S(2)}, u32[]{:S(2)}) collective-permute-start(f32[2,128,1024]{2,1,0:T(8,128)} %get-tuple-element.99), channel_id=1, source_target_pairs={{0,16},{8,24},{16,0},{24,8},{1,17},{9,25},{17,1},{25,9},{2,18},{10... | collective-permute-start | bytes 3145736 | tf_op jit(solution)/shard_map/ppermute | solution.py:339
  232.9 52.7 %collective-permute-start.8 = (f32[128,1024]{1,0:T(8,128)}, f32[128,1024]{1,0:T(8,128)S(1)}, u32[]{:S(2)}, u32[]{:S(2)}) collective-permute-start(f32[128,1024]{1,0:T(8,128)} %get-tuple-element.111), channel_id=1, source_target_pairs={{0,16},{8,24},{16,0},{24,8},{1,17},{9,25},{17,1},{25,9},{2,18},{10... | collective-permute-start | bytes 1572872 | tf_op jit(solution)/shard_map/ppermute | solution.py:339
  235.0 50.6 %collective-permute-start.9 = (f32[128,1024]{1,0:T(8,128)}, f32[128,1024]{1,0:T(8,128)S(1)}, u32[]{:S(2)}, u32[]{:S(2)}) collective-permute-start(f32[128,1024]{1,0:T(8,128)} %get-tuple-element.112), channel_id=1, source_target_pairs={{0,8},{8,0},{16,24},{24,16},{1,9},{9,1},{17,25},{25,17},{2,10},{10... | collective-permute-start | bytes 1572872 | tf_op jit(solution)/shard_map/ppermute | solution.py:339
  254.5 2.2 copy-start.4
  259.4 26.2 %collective-permute-start.10 = (f32[128,1024]{1,0:T(8,128)}, f32[128,1024]{1,0:T(8,128)S(1)}, u32[]{:S(2)}, u32[]{:S(2)}) collective-permute-start(f32[128,1024]{1,0:T(8,128)} %get-tuple-element.100), channel_id=1, source_target_pairs={{0,16},{8,24},{16,0},{24,8},{1,17},{9,25},{17,1},{25,9},{2,18},{10... | collective-permute-start | bytes 1572872 | tf_op jit(solution)/shard_map/ppermute | solution.py:339
  259.4 26.2 %collective-permute-start.11 = (f32[128,1024]{1,0:T(8,128)}, f32[128,1024]{1,0:T(8,128)S(1)}, u32[]{:S(2)}, u32[]{:S(2)}) collective-permute-start(f32[128,1024]{1,0:T(8,128)} %get-tuple-element.101), channel_id=1, source_target_pairs={{0,8},{8,0},{16,24},{24,16},{1,9},{9,1},{17,25},{25,17},{2,10},{10... | collective-permute-start | bytes 1572872 | tf_op jit(solution)/shard_map/ppermute | solution.py:339
  285.6 0.8 copy-start.11
  285.6 1.0 copy-start.12
  285.6 12.1 %copy-start.13 = (f32[128,1024]{1,0:T(8,128)}, f32[128,1024]{1,0:T(8,128)S(1)}, u32[]{:S(2)}) copy-start(f32[128,1024]{1,0:T(8,128)S(1)} %collective-permute-done.10.refs_3_) | copy-start | bytes 1572868
  285.6 12.1 %copy-start.14 = (f32[128,1024]{1,0:T(8,128)}, f32[128,1024]{1,0:T(8,128)S(1)}, u32[]{:S(2)}) copy-start(f32[128,1024]{1,0:T(8,128)S(1)} %collective-permute-done.11.refs_6_) | copy-start | bytes 1572868
  286.6 31.0 %collective-permute-start.12 = (f32[2,128,1024]{2,1,0:T(8,128)}, f32[2,128,1024]{2,1,0:T(8,128)S(1)}, u32[]{:S(2)}, u32[]{:S(2)}) collective-permute-start(f32[2,128,1024]{2,1,0:T(8,128)} %get-tuple-element.120), channel_id=1, source_target_pairs={{0,8},{8,0},{16,24},{24,16},{1,9},{9,1},{17,25},{25,17},{2,10},{10... | collective-permute-start | bytes 3145736 | tf_op jit(solution)/shard_map/ppermute | solution.py:339
  293.6 25.1 %collective-permute-start.13 = (f32[2,128,1024]{2,1,0:T(8,128)}, f32[2,128,1024]{2,1,0:T(8,128)S(1)}, u32[]{:S(2)}, u32[]{:S(2)}) collective-permute-start(f32[2,128,1024]{2,1,0:T(8,128)} %get-tuple-element.121), channel_id=1, source_target_pairs={{0,16},{8,24},{16,0},{24,8},{1,17},{9,25},{17,1},{25,9},{2,18},{10... | collective-permute-start | bytes 3145736 | tf_op jit(solution)/shard_map/ppermute | solution.py:339
  317.6 1.1 copy-start
  318.7 1.0 copy-start.1
  322.2 29.9 %collective-permute-start.14 = (f32[128,1024]{1,0:T(8,128)}, f32[128,1024]{1,0:T(8,128)S(1)}, u32[]{:S(2)}, u32[]{:S(2)}) collective-permute-start(f32[128,1024]{1,0:T(8,128)} %get-tuple-element.129), channel_id=1, source_target_pairs={{0,16},{8,24},{16,0},{24,8},{1,17},{9,25},{17,1},{25,9},{2,18},{10... | collective-permute-start | bytes 1572872 | tf_op jit(solution)/shard_map/ppermute | solution.py:339
  322.5 29.7 %collective-permute-start.15 = (f32[128,1024]{1,0:T(8,128)}, f32[128,1024]{1,0:T(8,128)S(1)}, u32[]{:S(2)}, u32[]{:S(2)}) collective-permute-start(f32[128,1024]{1,0:T(8,128)} %get-tuple-element.130), channel_id=1, source_target_pairs={{0,8},{8,0},{16,24},{24,16},{1,9},{9,1},{17,25},{25,17},{2,10},{10... | collective-permute-start | bytes 1572872 | tf_op jit(solution)/shard_map/ppermute | solution.py:339
  352.2 20.7 %copy-start.9 = (f32[128,1024]{1,0:T(8,128)}, f32[128,1024]{1,0:T(8,128)S(1)}, u32[]{:S(2)}) copy-start(f32[128,1024]{1,0:T(8,128)S(1)} %collective-permute-done.14.refs_3_) | copy-start | bytes 1572868
  352.2 20.7 %copy-start.10 = (f32[128,1024]{1,0:T(8,128)}, f32[128,1024]{1,0:T(8,128)S(1)}, u32[]{:S(2)}) copy-start(f32[128,1024]{1,0:T(8,128)S(1)} %collective-permute-done.15.refs_6_) | copy-start | bytes 1572868
  352.2 24.1 %collective-permute-start.16 = (f32[2,128,768]{2,1,0:T(8,128)}, f32[2,128,768]{2,1,0:T(8,128)S(1)}, u32[]{:S(2)}, u32[]{:S(2)}) collective-permute-start(f32[2,128,768]{2,1,0:T(8,128)} %get-tuple-element.141), channel_id=1, source_target_pairs={{0,8},{8,0},{16,24},{24,16},{1,9},{9,1},{17,25},{25,17},{2,10},{10... | collective-permute-start | bytes 2359304 | tf_op jit(solution)/shard_map/ppermute | solution.py:339
  359.2 19.7 %collective-permute-start.17 = (f32[2,128,768]{2,1,0:T(8,128)}, f32[2,128,768]{2,1,0:T(8,128)S(1)}, u32[]{:S(2)}, u32[]{:S(2)}) collective-permute-start(f32[2,128,768]{2,1,0:T(8,128)} %get-tuple-element.142), channel_id=1, source_target_pairs={{0,16},{8,24},{16,0},{24,8},{1,17},{9,25},{17,1},{25,9},{2,18},{10... | collective-permute-start | bytes 2359304 | tf_op jit(solution)/shard_map/ppermute | solution.py:339
  376.3 2.6 copy-start.5
  378.9 0.9 copy-start.6
  378.9 9.4 %collective-permute-start.18 = (f32[2,128,256]{2,1,0:T(8,128)}, f32[2,128,256]{2,1,0:T(8,128)S(1)}, u32[]{:S(2)}, u32[]{:S(2)}) collective-permute-start(f32[2,128,256]{2,1,0:T(8,128)} %get-tuple-element.144), channel_id=1, source_target_pairs={{0,8},{8,0},{16,24},{24,16},{1,9},{9,1},{17,25},{25,17},{2,10},{10... | collective-permute-start | bytes 786440 | tf_op jit(solution)/shard_map/ppermute | solution.py:339
  378.9 9.4 %collective-permute-start.19 = (f32[2,128,256]{2,1,0:T(8,128)}, f32[2,128,256]{2,1,0:T(8,128)S(1)}, u32[]{:S(2)}, u32[]{:S(2)}) collective-permute-start(f32[2,128,256]{2,1,0:T(8,128)} %get-tuple-element.146), channel_id=1, source_target_pairs={{0,16},{8,24},{16,0},{24,8},{1,17},{9,25},{17,1},{25,9},{2,18},{10... | collective-permute-start | bytes 786440 | tf_op jit(solution)/shard_map/ppermute | solution.py:339
  382.1 15.0 %collective-permute-start.22 = (f32[128,768]{1,0:T(8,128)}, f32[128,768]{1,0:T(8,128)S(1)}, u32[]{:S(2)}, u32[]{:S(2)}) collective-permute-start(f32[128,768]{1,0:T(8,128)} %get-tuple-element.154), channel_id=1, source_target_pairs={{0,16},{8,24},{16,0},{24,8},{1,17},{9,25},{17,1},{25,9},{2,18},{10... | collective-permute-start | bytes 1179656 | tf_op jit(solution)/shard_map/ppermute | solution.py:339
  383.2 13.8 %collective-permute-start.23 = (f32[128,768]{1,0:T(8,128)}, f32[128,768]{1,0:T(8,128)S(1)}, u32[]{:S(2)}, u32[]{:S(2)}) collective-permute-start(f32[128,768]{1,0:T(8,128)} %get-tuple-element.155), channel_id=1, source_target_pairs={{0,8},{8,0},{16,24},{24,16},{1,9},{9,1},{17,25},{25,17},{2,10},{10... | collective-permute-start | bytes 1179656 | tf_op jit(solution)/shard_map/ppermute | solution.py:339
  388.3 0.7 copy-start.7
  389.0 0.7 copy-start.8
  391.5 10.7 %collective-permute-start.20 = (f32[128,256]{1,0:T(8,128)}, f32[128,256]{1,0:T(8,128)S(1)}, u32[]{:S(2)}, u32[]{:S(2)}) collective-permute-start(f32[128,256]{1,0:T(8,128)} %get-tuple-element.147), channel_id=1, source_target_pairs={{0,16},{8,24},{16,0},{24,8},{1,17},{9,25},{17,1},{25,9},{2,18},{10... | collective-permute-start | bytes 393224 | tf_op jit(solution)/shard_map/ppermute | solution.py:339
  391.5 10.7 %collective-permute-start.21 = (f32[128,256]{1,0:T(8,128)}, f32[128,256]{1,0:T(8,128)S(1)}, u32[]{:S(2)}, u32[]{:S(2)}) collective-permute-start(f32[128,256]{1,0:T(8,128)} %get-tuple-element.148), channel_id=1, source_target_pairs={{0,8},{8,0},{16,24},{24,16},{1,9},{9,1},{17,25},{25,17},{2,10},{10... | collective-permute-start | bytes 393224 | tf_op jit(solution)/shard_map/ppermute | solution.py:339
  397.0 0.8 copy-start.15
  397.8 0.8 copy-start.16
  402.3 0.6 copy-start.17
  (1 other events, 0.6 us)
Sparse Core Ops, SparseCore 0:
  13.3 153.8 all-gather.6
  168.8 80.3 all-gather.8
  250.8 80.5 all-gather.10
